TPU v7x, 32 devices: a whole 2x2x4 slice. The times are simulated.
32 devices in a mesh: tiles: 8 (over z, y), rep: 4 (over x, core).
Axes of the slice: x: 2, y: 2, z: 4, core: 2. Of those that a mesh axis runs over, the one named last changes fastest.
Arguments:
- trailing_tiles: float32 [4800, 256, 256], P(('tiles', 'rep')), may hold values from -6 to 6
- panel_rows: float32 [96, 256, 512], P('tiles'), may hold values from -3 to 3
- pivot_blocks: float32 [2, 256, 256], replicated
- coupling: float32 [256, 256], replicated, may hold values from -0.1875 to 0.1875
- row_ids: int32 [96], replicated, may hold values from 2 to 96, as said below
- membership: int32 [8, 106], replicated, may hold values from 2 to 96, as said below
- tile_pairs: int32 [4800, 2], P(('tiles', 'rep')), may hold values from 0 to 106, as said below
Outputs:
- updated_tiles: float32 [4800, 256, 256], P(('tiles', 'rep'))
- factors: float32 [96, 256, 512], P('tiles')
- pivot_diag: float32 [2, 256], replicated
Inputs may be any that keep to these rules, and one draw needn't show every extreme that they name: `row_ids`: each row block 2 to 95 stands in exactly one slot; the other slots hold 96. `membership`: entries are row blocks 2 to 95, or 96 for none. `tile_pairs`: a slot's first entry is below 12, its second from 12 to 105, or both are 106 for an empty slot; over all devices every unordered pair of row blocks 2 to 96 - 1 (a block with itself too) is listed exactly once; some device fills all 150 slots.
All inputs are finite; a program needn't handle non-finite values.
Results may differ from a plain program's by a relative error of at most 0.00005.
Values sent between devices are 32-bit elements; how exact they have to be, the bound alone decides.
A program may use at most 384 MiB of HBM per device.

v0:
```python
import functools

import jax
import jax.numpy as jnp
from jax import lax
from jax.experimental import pallas as pl
from jax.experimental.pallas import tpu as pltpu
from jax.sharding import PartitionSpec as P

NB = 96
LEFT = 12
HI = lax.Precision.HIGHEST
MESH = pl.DeviceIdType.MESH
MINE, SHARED, OTHER = 0, 1, 2


def matmul(left, right, turned=False):
    return lax.dot_general(left, right, (((1,), (1 if turned else 0,)), ((), ())), precision=HI,
                           preferred_element_type=jnp.float32)


def pivot_stages(pivot_blocks, coupling, inverse, diagonal, work, lower, schur, solve, coupled):
    block = coupling.shape[0]
    h = block // 2
    quarter = h // 4

    def identity():
        return lax.broadcasted_iota(jnp.int32, (h, h), 0) == lax.broadcasted_iota(jnp.int32, (h, h), 1)

    def begin(matrix):
        work[:, :h] = matrix
        work[:, h:] = identity().astype(jnp.float32)

    def eliminate(part):
        first = part * quarter
        lane = lax.broadcasted_iota(jnp.int32, (h - first, h), 1)
        below = lax.broadcasted_iota(jnp.int32, (h - first, 1), 0) + first
        lane_row = lax.broadcasted_iota(jnp.int32, (1, h), 1)

        def step(j, carry):
            row = work[pl.ds(j, 1), :]
            rest = work[first:, :]
            column = jnp.sum(jnp.where(lane == j, rest[:, :h], 0.0), axis=1, keepdims=True)
            pivot = jnp.sum(jnp.where(lane_row == j, row[:, :h], 0.0), axis=1, keepdims=True)
            work[first:, :] = rest - jnp.where(below > j, column / pivot, 0.0) * row
            return carry

        lax.fori_loop(first, first + quarter, step, 0)

    def result():
        picked = jnp.where(identity(), work[:, :h], 0.0)
        return (work[:, h:], jnp.sum(picked, axis=0, keepdims=True), jnp.sum(picked, axis=1, keepdims=True))

    def pivot(at, source):
        base = at * block

        def middle():
            unit, d_row, d_column = result()
            zero = jnp.zeros((h, h), jnp.float32)
            solve[:h, :h] = unit
            solve[:h, h:] = zero
            inverse[base:base + h, base:base + h] = unit / d_column
            inverse[base:base + h, base + h:base + block] = zero
            diagonal[at:at + 1, :h] = d_row
            scaled = matmul(source()[h:, :h], unit, True)
            lower[...] = scaled / d_row
            begin(source()[h:, h:] - matmul(scaled, lower[...], True))

        def last():
            unit, d_row, d_column = result()
            corner = -matmul(matmul(unit, lower[...]), solve[:h, :h])
            solve[h:, :h] = corner
            solve[h:, h:] = unit
            inverse[base + h:base + block, base:base + h] = corner / d_column
            inverse[base + h:base + block, base + h:base + block] = unit / d_column
            diagonal[at:at + 1, h:] = d_row

        walk = [(5.5, functools.partial(eliminate, part)) for part in range(4)]
        return [(0.5, lambda: begin(source()[:h, :h]))] + walk + [(2, middle)] + walk + [(2, last)]

    def couple():
        coupled[...] = matmul(coupling[...], solve[...], True)
        schur[...] = pivot_blocks[1] - matmul(coupled[...], coupled[...] / diagonal[0:1, :], True)

    def join():
        inverse[:block, block:] = jnp.zeros((block, block), jnp.float32)
        mixed = matmul(inverse[block:, block:], coupled[...])
        inverse[block:, :block] = -matmul(mixed, inverse[:block, :block])

    return (pivot(0, lambda: pivot_blocks[0]) + [(3, couple)] + pivot(1, lambda: schur[...]) + [(3, join)])


def spread_kernel(sizes, panel, pivot_blocks, coupling, out, inverse, diagonal, factors,
                  z_send, z_recv, y_send, y_recv, x_send, x_recv, c_send, c_recv, own_sem,
                  work, lower, schur, solve, coupled, rows_in, rows_out, in_sem, out_sem):
    nz, rows, half, alone, shared = sizes
    tile, rep = lax.axis_index("tiles"), lax.axis_index("rep")
    z, y = tile // 2, tile % 2
    x, core = rep // 2, rep % 2
    items = [(0, 0)] + [(s, way) for s in range(1, nz) for way in (0, 1)]
    number = {item: at for at, item in enumerate(items)}

    def there(item):
        step, way = item
        if step == 0:
            return None
        return z - step >= 0 if way == 0 else z + step < nz

    def place(item):
        step, way = item
        return z - step if way == 0 else z + step

    def when(cond, body):
        if cond is None:
            body()
        else:
            pl.when(cond)(body)

    def both(a, b):
        return b if a is None else jnp.logical_and(a, b)

    def offset(part):
        if part == MINE:
            return core * half + x * (alone + shared), alone
        if part == SHARED:
            return core * half + alone, shared
        return core * half + (1 - x) * (alone + shared), alone

    def piece(column, item, part):
        start, size = offset(part)
        if column == 0 and item == (0, 0):
            return panel.at[pl.ds(pl.multiple_of(start, 8), size)]
        return landing(column, item, part)

    def landing(column, item, part):
        start, size = offset(part)
        owner = place(item) * 2 + (y if column == 0 else 1 - y)
        return out.at[pl.ds(pl.multiple_of(owner * rows + start, 8), size)]

    def copy(column, item, part, send, recv, target):
        return pltpu.make_async_remote_copy(
            src_ref=piece(column, item, part), dst_ref=landing(column, item, part),
            send_sem=send, recv_sem=recv, device_id=target, device_id_type=MESH,
        )

    def z_copy(step, way, part):
        at = ((step - 1) * 2 + way) * 2 + part
        item = (step - 1, way if step > 1 else 0)
        target = (tile + 2 if way == 0 else tile - 2, rep)
        return copy(0, item, part, z_send.at[at], z_recv.at[at], target)

    def z_sends(step, way):
        room = z + 1 < nz if way == 0 else z >= 1
        return both(there((step - 1, way)), room)

    def z_arrival(step, way, part):
        at = ((step - 1) * 2 + way) * 2 + part
        return copy(0, (step, way), part, z_send.at[at], z_recv.at[at], (tile, rep))

    def y_copy(column, item, part):
        at = number[item] * 2 + part
        return copy(column, item, part, y_send.at[at], y_recv.at[at], (z * 2 + 1 - y, rep))

    def x_copy(column, item, part=MINE):
        at = column * len(items) + number[item]
        return copy(column, item, part, x_send.at[at], x_recv.at[at], (tile, (1 - x) * 2 + core))

    def c_copy(column, item, part):
        at = (column * len(items) + number[item]) * 3 + part
        return copy(column, item, part, c_send.at[at], c_recv.at[at], (tile, x * 2 + 1 - core))

    def c_arrival(column, item, part):
        at = (column * len(items) + number[item]) * 3 + part
        start, size = offset(part)
        start = start + (1 - 2 * core) * half
        owner = place(item) * 2 + (y if column == 0 else 1 - y)
        ref = out.at[pl.ds(pl.multiple_of(owner * rows + start, 8), size)]
        return pltpu.make_async_remote_copy(
            src_ref=ref, dst_ref=ref, send_sem=c_send.at[at], recv_sem=c_recv.at[at],
            device_id=(tile, x * 2 + 1 - core), device_id_type=MESH,
        )

    barrier = pltpu.get_barrier_semaphore()

    def greet(target):
        pl.semaphore_signal(barrier, inc=1, device_id=target, device_id_type=MESH)

    greet((z * 2 + 1 - y, rep))
    greet((tile, (1 - x) * 2 + core))
    greet((tile, x * 2 + 1 - core))
    pl.when(z >= 1)(lambda: greet((tile - 2, rep)))
    pl.when(z + 1 < nz)(lambda: greet((tile + 2, rep)))
    peers = 3 + jnp.where(z >= 1, 1, 0) + jnp.where(z + 1 < nz, 1, 0)
    pl.semaphore_wait(barrier, peers)

    for part in (MINE, SHARED):
        for way in (0, 1):
            if nz > 1:
                when(z_sends(1, way), lambda: z_copy(1, way, part).start())
        y_copy(0, (0, 0), part).start()
    own = pltpu.make_async_copy(panel, out.at[pl.ds(pl.multiple_of(tile * rows, 8), rows)], own_sem)
    own.start()

    def on_z(step, way, part):
        item = (step, way)

        def body():
            z_arrival(step, way, part).wait_recv()
            if step + 1 < nz:
                when(z_sends(step + 1, way), lambda: z_copy(step + 1, way, part).start())
            y_copy(0, item, part).start()
            if part == MINE:
                x_copy(0, item).start()
            c_copy(0, item, part).start()

        when(there(item), body)

    def on_y(item, part):
        def body():
            y_copy(1, item, part).wait_recv()
            if part == MINE:
                x_copy(1, item).start()
            c_copy(1, item, part).start()

        when(there(item), body)

    def on_x(column, item):
        def body():
            x_copy(column, item, OTHER).wait_recv()
            c_copy(column, item, OTHER).start()

        when(there(item), body)

    def at_step(step):
        return [item for item in items if item[0] == step]

    block = rows_in.shape[0]

    def solve_rows(at):
        here = pl.ds(at * block, block)
        fetch = pltpu.make_async_copy(panel.at[here], rows_in, in_sem)
        fetch.start()
        fetch.wait()
        rows_out[...] = matmul(rows_in[...], inverse[...], True)
        store = pltpu.make_async_copy(rows_out, factors.at[here], out_sem)
        store.start()
        store.wait()

    stages = pivot_stages(pivot_blocks, coupling, inverse, diagonal, work, lower, schur, solve, coupled)
    stages += [(2.2, functools.partial(solve_rows, at)) for at in range(rows // block)]
    total = sum(weight for weight, _ in stages)
    done, gap = 0.0, 0

    def arithmetic():
        nonlocal done, gap
        gap += 1
        while stages and (done < total * gap / (2 * nz) or gap == 2 * nz):
            weight, stage = stages.pop(0)
            stage()
            done += weight

    for step in range(1, nz + 1):
        for part in (MINE, SHARED):
            arithmetic()
            if step < nz:
                for way in (0, 1):
                    on_z(step, way, part)
            for item in at_step(step - 1):
                on_y(item, part)
        if step < nz:
            for item in at_step(step - 1):
                if step > 1:
                    on_x(0, item)
            for item in at_step(step - 2):
                on_x(1, item)
    for item in at_step(nz - 1):
        on_x(0, item)
    for step in (nz - 2, nz - 1):
        for item in at_step(step):
            on_x(1, item)

    for column in (0, 1):
        for item in items:
            if column == 0 and item == (0, 0):
                continue

            def finish():
                for part in (MINE, SHARED, OTHER):
                    c_arrival(column, item, part).wait_recv()
                    c_copy(column, item, part).wait_send()
                x_copy(column, item).wait_send()

            when(there(item), finish)
    for item in items:
        for part in (MINE, SHARED):
            when(there(item), lambda: y_copy(0, item, part).wait_send())
            for way in (0, 1):
                if item[0] + 1 < nz and (item[0] == 0 or item[1] == way):
                    step = item[0] + 1
                    when(z_sends(step, way), lambda: z_copy(step, way, part).wait_send())
    own.wait()


def spread(panel, pivot_blocks, coupling, mesh):
    n_tiles, n_rep = mesh.shape["tiles"], mesh.shape["rep"]
    assert n_tiles % 2 == 0 and n_rep == 4
    nz = n_tiles // 2
    rows, width = panel.shape
    half = rows // 2
    alone = half // 24 * 8
    sizes = (nz, rows, half, alone, half - 2 * alone)
    n_items = 2 * nz - 1
    dma = lambda n: pltpu.SemaphoreType.DMA((n,))
    block = coupling.shape[0]
    any_space, vmem = pl.BlockSpec(memory_space=pl.ANY), pl.BlockSpec(memory_space=pltpu.VMEM)
    f32 = lambda *shape: jax.ShapeDtypeStruct(shape, jnp.float32)
    buffer = lambda *shape: pltpu.VMEM(shape, jnp.float32)
    return pl.pallas_call(
        functools.partial(spread_kernel, sizes),
        out_shape=(f32(n_tiles * rows, width), f32(width, width), f32(*pivot_blocks.shape[:2]), f32(rows, width)),
        in_specs=[any_space, vmem, vmem],
        out_specs=(any_space, vmem, vmem, any_space),
        scratch_shapes=[dma(4 * max(nz - 1, 1))] * 2 + [dma(2 * n_items)] * 2 + [dma(2 * n_items)] * 2
        + [dma(6 * n_items)] * 2 + [pltpu.SemaphoreType.DMA]
        + [buffer(block // 2, block), buffer(block // 2, block // 2)] + [buffer(block, block)] * 3
        + [buffer(block, width)] * 2 + [pltpu.SemaphoreType.DMA] * 2,
        compiler_params=pltpu.CompilerParams(
            collective_id=0, has_side_effects=True, vmem_limit_bytes=40 << 20),
        name="spread_rows",
    )(panel, pivot_blocks, coupling)


def halves(value):
    high = value.astype(jnp.bfloat16)
    low = (value - high.astype(jnp.float32)).astype(jnp.bfloat16)
    return high, low


def split_product(stacked, right, dims):
    rows = stacked.shape[0] // 2
    high, low = halves(right)
    dot = functools.partial(lax.dot_general, dimension_numbers=(dims, ((), ())), preferred_element_type=jnp.float32)
    first = dot(stacked, high)
    return first[:rows] + (first[rows:] + dot(stacked[:rows], low))


def left_kernel(source, rows, gram, out):
    stacked = jnp.concatenate(halves(rows[0]), axis=0)
    product = split_product(stacked, gram[...], ((1,), (0,)))
    out[0] = jnp.concatenate(halves(product), axis=0)


def left_rows(every_row, gram, source):
    block, width = every_row.shape[1:]
    return pl.pallas_call(
        left_kernel,
        grid_spec=pltpu.PrefetchScalarGridSpec(
            num_scalar_prefetch=1, grid=(source.shape[0],),
            in_specs=[
                pl.BlockSpec((1, block, width), lambda i, src: (src[i], 0, 0)),
                pl.BlockSpec((width, width), lambda i, src: (0, 0)),
            ],
            out_specs=pl.BlockSpec((1, 2 * block, width), lambda i, src: (i, 0, 0)),
        ),
        out_shape=jax.ShapeDtypeStruct((source.shape[0], 2 * block, width), jnp.bfloat16),
        compiler_params=pltpu.CompilerParams(vmem_limit_bytes=32 << 20),
        name="left_rows",
    )(source, every_row, gram)


def update_kernel(per_step, left, right, used, tiles, weights, *refs):
    rows, out = refs[:per_step], refs[per_step]
    step = pl.program_id(0)
    for at in range(per_step):
        slot = step * per_step + at
        product = split_product(weights[left[slot]], rows[at][0], ((1,), (1,)))
        out[at] = tiles[at] - jnp.where(used[slot] > 0, product, jnp.zeros_like(product))


def update(tiles, weights, every_row, left, right, used):
    slots, block, _ = tiles.shape
    width = every_row.shape[2]
    per_step = next(n for n in (5, 4, 3, 2, 1) if slots % n == 0)
    row_spec = lambda at: pl.BlockSpec((1, block, width), lambda i, l, r, u: (r[i * per_step + at], 0, 0))
    tile_spec = pl.BlockSpec((per_step, block, block), lambda i, l, r, u: (i, 0, 0))
    return pl.pallas_call(
        functools.partial(update_kernel, per_step),
        grid_spec=pltpu.PrefetchScalarGridSpec(
            num_scalar_prefetch=3, grid=(slots // per_step,),
            in_specs=[tile_spec, pl.BlockSpec(weights.shape, lambda i, l, r, u: (0, 0, 0))]
            + [row_spec(at) for at in range(per_step)],
            out_specs=tile_spec,
        ),
        out_shape=jax.ShapeDtypeStruct(tiles.shape, tiles.dtype),
        compiler_params=pltpu.CompilerParams(vmem_limit_bytes=56 << 20),
        name="update_tiles",
    )(left, right, used, tiles, weights, *[every_row] * per_step)


def per_device(mesh, trailing_tiles, panel_rows, pivot_blocks, coupling, row_ids, membership, tile_pairs):
    owned, block, width = panel_rows.shape
    tile_index = lax.axis_index("tiles")
    own_ids = lax.dynamic_slice_in_dim(row_ids, tile_index * owned, owned)
    wanted = lax.dynamic_index_in_dim(membership, tile_index, 0, keepdims=False)
    source = jnp.argmax(row_ids[None, :] == wanted[:, None], axis=1).astype(jnp.int32)
    listed = jnp.concatenate([wanted < NB, jnp.zeros((1,), bool)])
    source = jnp.concatenate([source, jnp.zeros((1,), jnp.int32)])
    left, right = tile_pairs[:, 0], tile_pairs[:, 1]
    used = (listed[left] & listed[right]).astype(jnp.int32)
    every_row, inverse, diagonal, factors = spread(
        panel_rows.reshape(owned * block, width), pivot_blocks, coupling, mesh)
    every_row = every_row.reshape(-1, block, width)
    factors = factors.reshape(panel_rows.shape)
    factors = jnp.where((own_ids < NB)[:, None, None], factors, jnp.zeros_like(factors))
    gram = jnp.dot((inverse * diagonal.reshape(-1, 1)).T, inverse, precision=HI)
    weights = left_rows(every_row, gram, source[:LEFT])
    updated = update(trailing_tiles, weights, every_row, jnp.minimum(left, LEFT - 1), source[right], used)
    return (updated, factors, diagonal)


def solution(mesh):
    return jax.shard_map(
        functools.partial(per_device, mesh),
        mesh=mesh,
        in_specs=(
            P(("tiles", "rep"), None, None),
            P("tiles", None, None),
            P(),
            P(),
            P(),
            P(),
            P(("tiles", "rep"), None),
        ),
        out_specs=(P(("tiles", "rep"), None, None), P("tiles", None, None), P()),
        check_vma=False,
    )
```

profile of v0, /device:TPU:13, one launch (start us, length us, event | category | flops | bytes accessed | tf_op | source)
XLA Modules:
  0.0 305.7 jit_solution(7928114990184521582)
XLA Ops:
  0.6 0.7 dynamic-slice_compare_fusion
  1.4 0.7 broadcast_compare_fusion
  2.1 0.1 pad_add_fusion
  2.1 1.3 iota_reduce_fusion
  3.4 0.1 pad_add_fusion.1
  3.5 1.3 compare_select_fusion
  4.8 1.6 gather_fusion.2
  6.4 2.1 gather_fusion
  8.5 1.6 gather_fusion.1
  10.1 0.6 and_convert_fusion.used
  10.6 0.0 copy-start.1
  10.7 2.8 copy-done.1
  13.4 0.0 copy-start.2
  13.4 1.0 copy-done.2
  14.5 0.0 copy-start.3
  14.5 0.9 copy-done.3
  15.4 202.2 %spread_rows.1 = (f32[24576,512]{1,0:T(8,128)}, f32[512,512]{1,0:T(8,128)S(1)}, f32[2,256]{1,0:T(2,128)S(1)}, f32[3072,512]{1,0:T(8,128)S(1)}) custom-call(f32[3072,512]{1,0:T(8,128)S(1)} %bitcast.13, f32[2,256,256]{2,1,0:T(8,128)S(1)} %copy-done.2, f32[256,256]{1,0:T(8,128)S(1)} %copy-done.3), custom_call_target="tpu_custom_call" | custom-call | tf_op jit(solution)/shard_map/spread_rows/pallas_call | solution.py:318
  217.7 2.0 fusion.gram
  219.7 11.3 %left_rows.1.weights = bf16[12,512,512]{2,1,0:T(8,128)(2,1)S(1)} custom-call(s32[12]{0:T(128)S(1)} %bitcast.16, f32[96,256,512]{2,1,0:T(8,128)} %bitcast.17, f32[512,512]{1,0:T(8,128)S(1)} %fusion.gram), custom_call_target="tpu_custom_call" | custom-call | tf_op jit(solution)/shard_map/left_rows/pallas_call | solution.py:355
  231.0 0.0 copy-start
  231.0 2.7 copy-done
  233.7 67.9 %update_tiles.1 = f32[150,256,256]{2,1,0:T(8,128)} custom-call(s32[150]{0:T(256)} %bitcast.26, s32[150]{0:T(256)} %gather_fusion, s32[150]{0:T(256)} %and_convert_fusion.used, f32[150,256,256]{2,1,0:T(8,128)} %tiles.1, bf16[12,512,512]{2,1,0:T(8,128)(2,1)} %copy-done, f32[96,256,512]{2,1,0:T(8,128)} %bitcast.18, f32[96,256,512]{2,1,0:T(8,128)} %bitcast.19, ...), custom_call_target="tpu_custom_call" | custom-call | tf_op jit(solution)/shard_map/update_tiles/pallas_call | solution.py:386
  301.6 3.6 %broadcast_select_fusion = f32[12,256,512]{2,1,0:T(8,128)} fusion(f32[12,256,512]{2,1,0:T(8,128)S(1)} %bitcast.14, pred[12]{0:T(512)(128)(4,1)S(1)} %dynamic-slice_compare_fusion), kind=kLoop, calls=%fused_computation.3 | loop fusion | flops 1572864 | bytes 12582924 | tf_op jit(solution)/shard_map/jit(_where)/select_n | solution.py:414
  305.2 0.6 copy.12
  (3 shorter events, 0.0 us)
Async XLA Ops:
  10.6 2.8 copy-start.1
  13.4 1.0 copy-start.2
  14.5 0.9 copy-start.3
  231.0 2.7 copy-start
where the time goes:
time: 308 us; the launch traced here: 306 us
  Pallas kernels  281 us (91%)
  local copies, waits for them, and re-layouts  13.3 us (4%)
  other arithmetic  8.37 us (3%)
    pallas_call x1, Pallas kernels, spread(): pl.pallas_call(functools.partial(spread_kernel, sizes), out_shape=(f32(n_...  202 us
    pallas_call x1, Pallas kernels, update(): pl.pallas_call(functools.partial(update_kernel, per_step), grid_spec=pltp...  67.9 us
    pallas_call x1, Pallas kernels, left_rows(): pl.pallas_call(left_kernel, grid_spec=pltpu.PrefetchScalarGridSpec(num_sc...  11.3 us
    unnamed x10, local copies, waits for them, and re-layouts  8.05 us

commit v1 on v0

--- a/solution.py
+++ b/solution.py
@@ -307,7 +307,7 @@
     nz = n_tiles // 2
     rows, width = panel.shape
     half = rows // 2
-    alone = half // 24 * 8
+    alone = half // 48 * 17 // 8 * 8
     sizes = (nz, rows, half, alone, half - 2 * alone)
     n_items = 2 * nz - 1
     dma = lambda n: pltpu.SemaphoreType.DMA((n,))
@@ -344,57 +344,63 @@
     return first[:rows] + (first[rows:] + dot(stacked[:rows], low))
 
 
-def left_kernel(source, rows, gram, out):
-    stacked = jnp.concatenate(halves(rows[0]), axis=0)
-    product = split_product(stacked, gram[...], ((1,), (0,)))
-    out[0] = jnp.concatenate(halves(product), axis=0)
-
-
-def left_rows(every_row, gram, source):
-    block, width = every_row.shape[1:]
-    return pl.pallas_call(
-        left_kernel,
-        grid_spec=pltpu.PrefetchScalarGridSpec(
-            num_scalar_prefetch=1, grid=(source.shape[0],),
-            in_specs=[
-                pl.BlockSpec((1, block, width), lambda i, src: (src[i], 0, 0)),
-                pl.BlockSpec((width, width), lambda i, src: (0, 0)),
-            ],
-            out_specs=pl.BlockSpec((1, 2 * block, width), lambda i, src: (i, 0, 0)),
-        ),
-        out_shape=jax.ShapeDtypeStruct((source.shape[0], 2 * block, width), jnp.bfloat16),
-        compiler_params=pltpu.CompilerParams(vmem_limit_bytes=32 << 20),
-        name="left_rows",
-    )(source, every_row, gram)
-
-
-def update_kernel(per_step, left, right, used, tiles, weights, *refs):
-    rows, out = refs[:per_step], refs[per_step]
+def update_kernel(per_step, pairs, source, tiles, gram, every_row, *refs):
+    rows, (out, weights, raw, sems) = refs[:per_step], refs[per_step:]
     step = pl.program_id(0)
+
+    @pl.when(step == 0)
+    def _():
+        def fetch(at):
+            return pltpu.make_async_copy(every_row.at[jnp.maximum(source[at], 0)], raw.at[at], sems.at[at])
+
+        for at in range(LEFT):
+            fetch(at).start()
+        weights[LEFT] = jnp.zeros(weights.shape[1:], weights.dtype)
+
+        def make(at, carry):
+            fetch(at).wait()
+            stacked = jnp.concatenate(halves(raw[at]), axis=0)
+            product = split_product(stacked, gram[...], ((1,), (0,)))
+            weights[at] = jnp.concatenate(halves(product), axis=0)
+            return carry
+
+        lax.fori_loop(0, LEFT, make, 0)
+
     for at in range(per_step):
         slot = step * per_step + at
-        product = split_product(weights[left[slot]], rows[at][0], ((1,), (1,)))
-        out[at] = tiles[at] - jnp.where(used[slot] > 0, product, jnp.zeros_like(product))
-
-
-def update(tiles, weights, every_row, left, right, used):
+        left, right = pairs[2 * slot], pairs[2 * slot + 1]
+        used = jnp.logical_and(source[left] >= 0, source[right] >= 0)
+        chosen = jnp.where(used, jnp.minimum(left, LEFT), LEFT)
+        out[at] = tiles[at] - split_product(weights[chosen], rows[at][0], ((1,), (1,)))
+
+
+def update(tiles, gram, every_row, pairs, source):
     slots, block, _ = tiles.shape
     width = every_row.shape[2]
     per_step = next(n for n in (5, 4, 3, 2, 1) if slots % n == 0)
-    row_spec = lambda at: pl.BlockSpec((1, block, width), lambda i, l, r, u: (r[i * per_step + at], 0, 0))
-    tile_spec = pl.BlockSpec((per_step, block, block), lambda i, l, r, u: (i, 0, 0))
+
+    def row_spec(at):
+        def place(i, pairs, source):
+            return jnp.maximum(source[pairs[2 * (i * per_step + at) + 1]], 0), 0, 0
+
+        return pl.BlockSpec((1, block, width), place)
+
+    tile_spec = pl.BlockSpec((per_step, block, block), lambda i, p, s: (i, 0, 0))
     return pl.pallas_call(
         functools.partial(update_kernel, per_step),
         grid_spec=pltpu.PrefetchScalarGridSpec(
-            num_scalar_prefetch=3, grid=(slots // per_step,),
-            in_specs=[tile_spec, pl.BlockSpec(weights.shape, lambda i, l, r, u: (0, 0, 0))]
-            + [row_spec(at) for at in range(per_step)],
+            num_scalar_prefetch=2, grid=(slots // per_step,),
+            in_specs=[tile_spec, pl.BlockSpec((width, width), lambda i, p, s: (0, 0)),
+                      pl.BlockSpec(memory_space=pl.ANY)] + [row_spec(at) for at in range(per_step)],
             out_specs=tile_spec,
+            scratch_shapes=[pltpu.VMEM((LEFT + 1, 2 * block, width), jnp.bfloat16),
+                            pltpu.VMEM((LEFT, block, width), jnp.float32),
+                            pltpu.SemaphoreType.DMA((LEFT,))],
         ),
         out_shape=jax.ShapeDtypeStruct(tiles.shape, tiles.dtype),
-        compiler_params=pltpu.CompilerParams(vmem_limit_bytes=56 << 20),
+        compiler_params=pltpu.CompilerParams(vmem_limit_bytes=48 << 20),
         name="update_tiles",
-    )(left, right, used, tiles, weights, *[every_row] * per_step)
+    )(pairs, source, tiles, gram, every_row, *[every_row] * per_step)
 
 
 def per_device(mesh, trailing_tiles, panel_rows, pivot_blocks, coupling, row_ids, membership, tile_pairs):
@@ -402,19 +408,15 @@
     tile_index = lax.axis_index("tiles")
     own_ids = lax.dynamic_slice_in_dim(row_ids, tile_index * owned, owned)
     wanted = lax.dynamic_index_in_dim(membership, tile_index, 0, keepdims=False)
-    source = jnp.argmax(row_ids[None, :] == wanted[:, None], axis=1).astype(jnp.int32)
-    listed = jnp.concatenate([wanted < NB, jnp.zeros((1,), bool)])
-    source = jnp.concatenate([source, jnp.zeros((1,), jnp.int32)])
-    left, right = tile_pairs[:, 0], tile_pairs[:, 1]
-    used = (listed[left] & listed[right]).astype(jnp.int32)
+    found = jnp.argmax(row_ids[None, :] == wanted[:, None], axis=1).astype(jnp.int32)
+    source = jnp.pad(jnp.where(wanted < NB, found, -1), (0, 1), constant_values=-1)
     every_row, inverse, diagonal, factors = spread(
         panel_rows.reshape(owned * block, width), pivot_blocks, coupling, mesh)
     every_row = every_row.reshape(-1, block, width)
     factors = factors.reshape(panel_rows.shape)
     factors = jnp.where((own_ids < NB)[:, None, None], factors, jnp.zeros_like(factors))
     gram = jnp.dot((inverse * diagonal.reshape(-1, 1)).T, inverse, precision=HI)
-    weights = left_rows(every_row, gram, source[:LEFT])
-    updated = update(trailing_tiles, weights, every_row, jnp.minimum(left, LEFT - 1), source[right], used)
+    updated = update(trailing_tiles, gram, every_row, tile_pairs.reshape(-1), source)
     return (updated, factors, diagonal)
 
 

time: 308 us -> 292 us (0.948)
  local copies, waits for them, and re-layouts: 13.3 us -> 6.97 us
  Pallas kernels: 281 us -> 275 us
    pallas_call x1 -> x0, Pallas kernels: 11.3 us -> none  [left_rows(): pl.pallas_call(left_kernel, grid_spec=pltpu.PrefetchScalarGridSpec(num_sc...]
    pallas_call x1, Pallas kernels: 67.9 us -> 74.8 us  [update(): pl.pallas_call(functools.partial(update_kernel, per_step), grid_spec=pltp...]
    gather x3 -> x0, local copies, waits for them, and re-layouts: 5.23 us -> none  [the longest x2 3.11 us: per_device(): used = (listed[left] & listed[right]).astype(jnp.int32)]
    unnamed x10 -> x9, local copies, waits for them, and re-layouts: 8.05 us -> 6.13 us
where the time goes in v1:
time: 292 us; the launch traced here: 291 us
  Pallas kernels  275 us (94%)
  local copies, waits for them, and re-layouts  6.97 us (2%)
  other arithmetic  6.25 us (2%)
    pallas_call x1, Pallas kernels, spread(): pl.pallas_call(functools.partial(spread_kernel, sizes), out_shape=(f32(n_...  200 us
    pallas_call x1, Pallas kernels, update(): pl.pallas_call(functools.partial(update_kernel, per_step), grid_spec=pltp...  74.8 us
    unnamed x9, local copies, waits for them, and re-layouts  6.13 us

profile of v1, /device:TPU:13, one launch (start us, length us, event | category | flops | bytes accessed | tf_op | source)
XLA Modules:
  0.0 290.7 jit_solution(15293108992940434489)
XLA Ops:
  0.6 0.7 dynamic-slice_compare_fusion
  1.4 0.7 dynamic-slice_bitcast_fusion
  2.1 1.3 iota_reduce_fusion
  3.3 0.7 compare_select_fusion
  4.0 0.8 copy.11
  4.8 0.1 reshape.24.pairs
  5.0 0.0 copy-start
  5.0 2.8 copy-done
  7.7 0.0 copy-start.1
  7.8 1.0 copy-done.1
  8.8 0.0 copy-start.2
  8.8 0.9 copy-done.2
  9.7 200.0 %spread_rows.1 = (f32[24576,512]{1,0:T(8,128)}, f32[512,512]{1,0:T(8,128)S(1)}, f32[2,256]{1,0:T(2,128)S(1)}, f32[3072,512]{1,0:T(8,128)S(1)}) custom-call(f32[3072,512]{1,0:T(8,128)S(1)} %bitcast.10, f32[2,256,256]{2,1,0:T(8,128)S(1)} %copy-done.1, f32[256,256]{1,0:T(8,128)S(1)} %copy-done.2), custom_call_target="tpu_custom_call" | custom-call | tf_op jit(solution)/shard_map/spread_rows/pallas_call | solution.py:318
  209.8 2.0 fusion.gram
  211.8 74.8 %update_tiles.1 = f32[150,256,256]{2,1,0:T(8,128)} custom-call(s32[300]{0:T(512)S(1)} %reshape.24.pairs, s32[107]{0:T(128)S(1)} %pad.4.source, f32[150,256,256]{2,1,0:T(8,128)} %tiles.1, f32[512,512]{1,0:T(8,128)S(1)} %fusion.gram, f32[96,256,512]{2,1,0:T(8,128)} %bitcast.13, f32[96,256,512]{2,1,0:T(8,128)} %bitcast.14, f32[96,256,512]{2,1,0:T(8,128)} %bitcast.15, ...), custom_call_target="tpu_custom_call" | custom-call | tf_op jit(solution)/shard_map/update_tiles/pallas_call | solution.py:389
  286.5 3.6 %broadcast_select_fusion = f32[12,256,512]{2,1,0:T(8,128)} fusion(f32[12,256,512]{2,1,0:T(8,128)S(1)} %bitcast.11, pred[12]{0:T(512)(128)(4,1)S(1)} %dynamic-slice_compare_fusion), kind=kLoop, calls=%fused_computation | loop fusion | flops 1572864 | bytes 12582924 | tf_op jit(solution)/shard_map/jit(_where)/select_n | solution.py:417
  290.1 0.6 copy.14
  (2 shorter events, 0.0 us)
Async XLA Ops:
  5.0 2.8 copy-start
  7.7 1.0 copy-start.1
  8.8 0.9 copy-start.2
